TPU v7x, 32 devices: a whole 2x2x4 slice. The times are simulated.
32 devices in a mesh: lon: 4 (over y, x), lat: 8 (over z, core).
Axes of the slice: x: 2, y: 2, z: 4, core: 2. Of those that a mesh axis runs over, the one named last changes fastest.
Arguments:
- sensitivity: float32 [32, 1440, 128], P('lat', 'lon'), may hold values from -6 to 6
- courant_east: float32 [32, 1440, 32], P('lat', 'lon'), may hold values from -0.9 to 0.9
- courant_north: float32 [32, 1440, 32], P('lat', 'lon'), may hold values from -0.9 to 0.9
- mixing: float32 [32, 1440, 31], P('lat', 'lon'), may hold values from 0.05 to 5
- cutoff: int32 [32], P('lat'), may hold values from 4 to 359
- polar_flag: int32 [32], P('lat'), may hold values from 0 to 1, as said below
Outputs:
- adjoint_out: float32 [32, 1440, 128], P('lat', 'lon')
Inputs may be any that keep to these rules, and one draw needn't show every extreme that they name: polar_flag is 1 on a run of rows starting at row 0 and on a run ending at row 31, each of 1 to 8 rows and one of them exactly 8, and 0 elsewhere.
All inputs are finite; a program needn't handle non-finite values.
Results may differ from a plain program's by a relative error of at most 0.0003.
Values sent between devices are 32-bit elements; how exact they have to be, the bound alone decides.
No kernel may reach another device: no remote copies, remote signals or barrier semaphores. Data moves between devices by JAX's collectives and lax.ppermute only.
A program may use at most 64 MiB of HBM per device.

v0:
```python
from functools import partial
import math
import jax
import jax.numpy as jnp
from jax import lax
from jax.sharding import PartitionSpec as P

SUBSTEPS = 2


def partner(block, axis, stride):
    count = lax.axis_size(axis)
    route = []
    for low in range(count):
        high = low | 1 << stride
        if high != low and high < count:
            route += [(low, high), (high, low)]
    return lax.ppermute(block, axis, route)


def padded_2(value, sides, width, wrap):
    for axis, dim in sides:
        count, length = (lax.axis_size(axis), value.shape[dim])
        up = [(i, (i + 1) % count) for i in range(count if wrap else count - 1)]
        down = [(j, i) for i, j in up]
        last = lax.slice_in_dim(value, length - width, length, axis=dim)
        initial = lax.slice_in_dim(value, 0, width, axis=dim)
        before = lax.ppermute(last, axis, up)
        after = lax.ppermute(initial, axis, down)
        value = jnp.concatenate([before, value, after], axis=dim)
    return value


def edge_row(offset):
    row = [0.0] * 6
    row[offset + 2] += 7.0 / 12.0
    row[offset + 3] += 7.0 / 12.0
    row[offset + 1] -= 1.0 / 12.0
    row[offset + 4] -= 1.0 / 12.0
    return row


def flux_weights(courant):
    left_edge = edge_row(-1)
    middle_edge = edge_row(0)
    right_edge = edge_row(1)
    magnitude = jnp.abs(courant)
    result = []
    for position in range(6):
        cell_plus = 1.0 if position == 2 else 0.0
        cell_minus = 1.0 if position == 3 else 0.0
        delta_plus = middle_edge[position] - left_edge[position]
        curve_plus = 6.0 * (cell_plus - 0.5 * (left_edge[position] + middle_edge[position]))
        delta_minus = right_edge[position] - middle_edge[position]
        curve_minus = 6.0 * (cell_minus - 0.5 * (middle_edge[position] + right_edge[position]))
        bend = 1.0 - 2.0 * magnitude / 3.0
        forward_weight = middle_edge[position] - 0.5 * magnitude * (delta_plus - bend * curve_plus)
        backward_weight = middle_edge[position] + 0.5 * magnitude * (
            delta_minus + bend * curve_minus
        )
        result.append(courant * jnp.where(courant >= 0.0, forward_weight, backward_weight))
    return result


def spread_flux(field_ext, courant_ext, axis_dim):
    length = field_ext.shape[axis_dim]
    jump = lax.slice_in_dim(field_ext, 1, length, axis=axis_dim) - lax.slice_in_dim(
        field_ext, 0, length - 1, axis=axis_dim
    )
    weights = flux_weights(lax.slice_in_dim(courant_ext, 0, length - 1, axis=axis_dim))
    padding = [(0, 0)] * jump.ndim
    padding[axis_dim] = (3, 3)
    total = jnp.zeros(field_ext.shape, field_ext.dtype)
    for position in range(6):
        offset = position - 2
        term = jnp.pad(weights[position] * jump, padding)
        total = total + lax.slice_in_dim(term, 3 - offset, 3 - offset + length, axis=axis_dim)
    return total


def solve_setup(mixing, tracers):
    rows, cols, interfaces = mixing.shape
    levels = interfaces + 1
    coef = jnp.moveaxis(mixing, 2, 0)
    nothing = jnp.zeros_like(coef[:1])
    padded = jnp.concatenate([nothing, coef, nothing], axis=0)
    beneath = -padded[:levels]
    overlying = -padded[1:]
    central = 1.0 - beneath - overlying
    factor_prev = jnp.zeros_like(coef[0])
    factor_list = []
    divisor_list = []
    for level in range(levels):
        divisor = central[level] - beneath[level] * factor_prev
        factor = overlying[level] / divisor
        factor_list.append(factor)
        divisor_list.append(divisor)
        factor_prev = factor

    def spread_lanes(values):
        return jnp.broadcast_to(values[..., None], (levels, rows, cols, tracers)).reshape(
            levels, rows * cols * tracers
        )

    return (
        spread_lanes(beneath),
        spread_lanes(jnp.stack(factor_list)),
        spread_lanes(jnp.stack(divisor_list)),
    )


def vertical_apply(field, coeffs, levels):
    rows, cols, channels = field.shape
    tracers = channels // levels
    beneath, factors, divisors = coeffs
    stack = (
        field.reshape(rows, cols, levels, tracers)
        .transpose(2, 0, 1, 3)
        .reshape(levels, rows * cols * tracers)
    )
    partial_prev = jnp.zeros_like(stack[0])
    partials = []
    for level in range(levels):
        partial_now = (stack[level] - beneath[level] * partial_prev) / divisors[level]
        partials.append(partial_now)
        partial_prev = partial_now
    following = jnp.zeros_like(stack[0])
    solved = [None] * levels
    for level in range(levels - 1, -1, -1):
        current = partials[level] - factors[level] * following
        solved[level] = current
        following = current
    result = jnp.stack(solved).reshape(levels, rows, cols, tracers).transpose(1, 2, 0, 3)
    return result.reshape(rows, cols, channels)


def fourier_table(circle):
    halfway = circle // 2
    places = jnp.arange(circle, dtype=jnp.int32)
    columns = jnp.arange(circle, dtype=jnp.int32)
    waves = columns % halfway
    phase = places[:, None] * waves[None, :] % circle
    angle = phase.astype(jnp.float32) * (2.0 * math.pi / circle)
    return jnp.where(columns[None, :] < halfway, jnp.cos(angle), jnp.sin(angle))


def local_setting(cutoff, polar_flag, lat_rows, channels, row_index):
    lat_local = row_index // channels
    chosen = lat_local[:, None] == jnp.arange(lat_rows, dtype=jnp.int32)[None, :]
    row_cut = jnp.sum(jnp.where(chosen, cutoff[None, :], 0), axis=1)
    row_flag = jnp.sum(jnp.where(chosen, polar_flag[None, :], 0), axis=1)
    return (row_cut, row_flag)


def filter_rows(rows, setting, table):
    circles = lax.all_to_all(rows, "lon", split_axis=0, concat_axis=1, tiled=True)
    count = circles.shape[0]
    row_index = lax.axis_index("lon") * count + jnp.arange(count, dtype=jnp.int32)
    row_cut, row_flag = setting(row_index)
    circle = table.shape[0]
    halfway = table.shape[1] // 2
    columns = jnp.arange(table.shape[1], dtype=jnp.int32)
    waves = columns % halfway
    is_sine = columns >= halfway
    scaling = jnp.where(waves == 0, 1.0, 2.0) / circle
    spectra = jnp.dot(
        circles, table, precision=lax.Precision.HIGHEST, preferred_element_type=jnp.float32
    )
    active = (waves[None, :] <= row_cut[:, None]) & jnp.logical_not(is_sine & (waves == 0))[None, :]
    weighted = jnp.where(active, spectra * scaling[None, :], 0.0)
    smooth = lax.dot_general(
        weighted,
        table,
        (((1,), (1,)), ((), ())),
        precision=lax.Precision.HIGHEST,
        preferred_element_type=jnp.float32,
    )
    mixed = jnp.where((row_flag > 0)[:, None], smooth, circles)
    return lax.all_to_all(mixed, "lon", split_axis=1, concat_axis=0, tiled=True)


def widen(courant, tracers):
    return jnp.repeat(courant, tracers, axis=2)


def meridional_core(field_ext, courant_ext, lat_first, lat_total):
    length = field_ext.shape[0]
    face_index = lat_first - 3 + jnp.arange(length, dtype=jnp.int32)
    valid = (face_index >= 0) & (face_index <= lat_total - 2)
    courant_ext = jnp.where(valid[:, None, None], courant_ext, 0.0)
    full = spread_flux(field_ext, courant_ext, 0)
    result = field_ext[3 : length - 3] + full[3 : length - 3]
    ghosts = jnp.concatenate([full[0:3], full[length - 3 :]], axis=0)
    arrived = partner(ghosts, "lon", lax.axis_size("lon").bit_length() - 2)
    lat_index = lax.axis_index("lat")
    south = jnp.where(lat_index == 0, arrived[2::-1], 0.0)
    north = jnp.where(lat_index == lax.axis_size("lat") - 1, arrived[5:2:-1], 0.0)
    result = result.at[0:3].add(south)
    result = result.at[result.shape[0] - 3 :].add(north)
    return result


def on_device(sensitivity, courant_east, courant_north, mixing, cutoff, polar_flag):
    lat_rows, lon_cols, channels = sensitivity.shape
    levels = courant_east.shape[2]
    tracers = channels // levels
    lat_total = lat_rows * lax.axis_size("lat")
    lat_first = lax.axis_index("lat") * lat_rows
    table = fourier_table(lon_cols * lax.axis_size("lon"))
    coeffs = solve_setup(mixing, tracers)
    state = sensitivity
    for substep in range(SUBSTEPS):
        state = vertical_apply(state, coeffs, levels)
        rows = state.transpose(0, 2, 1).reshape(lat_rows * channels, lon_cols)
        setting = partial(local_setting, cutoff, polar_flag, lat_rows, channels)
        state = (
            filter_rows(rows, setting, table)
            .reshape(lat_rows, channels, lon_cols)
            .transpose(0, 2, 1)
        )
        stacked = jnp.concatenate([state, courant_north], axis=2)
        margin = padded_2(stacked, (("lat", 0),), 3, False)
        northward = meridional_core(
            margin[:, :, :channels], widen(margin[:, :, channels:], tracers), lat_first, lat_total
        )
        stacked = jnp.concatenate([northward, courant_east], axis=2)
        margin = padded_2(stacked, (("lon", 1),), 3, True)
        northward = margin[:, :, :channels]
        east_courant = widen(margin[:, :, channels:], tracers)
        state = northward[:, 3:-3] + spread_flux(northward, east_courant, 1)[:, 3:-3]
    return state


def solution(mesh):
    return jax.shard_map(
        on_device,
        mesh=mesh,
        in_specs=(
            P("lat", "lon", None),
            P("lat", "lon", None),
            P("lat", "lon", None),
            P("lat", "lon", None),
            P("lat"),
            P("lat"),
        ),
        out_specs=P("lat", "lon", None),
        check_vma=False,
    )
```

profile of v0, /device:TPU:9, one launch (start us, length us, event | category | flops | bytes accessed | tf_op | source)
XLA Modules:
  0.0 415.6 jit_solution(10514916888348440577)
XLA Ops:
  0.0 1.1 fusion.232
  2.2 0.7 fusion.169
  2.9 0.6 fusion.168
  3.6 0.6 fusion.170
  4.2 0.6 fusion.172
  4.8 0.6 fusion.174
  5.5 0.6 fusion.176
  6.2 1.6 constant_dynamic-update-slice_fusion.31
  8.7 1.2 copy.40
  9.9 4.0 all-to-all-start
  13.9 38.1 %sine_select_fusion.22 = f32[1440,1440]{1,0:T(8,128)} fusion(s32[1440]{0:T(1024)S(1)} %add_select_fusion.1, pred[1440]{0:T(1024)(128)(4,1)S(1)} %get-tuple-element.259), kind=kLoop, calls=%fused_computation.3.clone.3.clone.clone.clone.clone.clone | loop fusion | flops 20736000 | bytes 8301600 | tf_op jit(solution)/shard_map/dot_general | solution.py:166
  52.7 18.1 %fusion.18 = f32[128,1440]{0,1:T(8,128)S(1)} fusion(f32[128,1440]{0,1:T(8,128)S(1)} %bitcast.221, s32[1440]{0:T(1024)S(1)} %add_select_fusion.1, f32[1440]{0:T(1024)S(1)} %select_multiply_fusion, s32[128]{0:T(128)S(1)} %get-tuple-element.54, pred[1440]{0:T(1024)(128)(4,1)S(1)} %get-tuple-element.260, f32[1440,1440]{1,0:T(8,128)} %sine_select_fusion.22), kind=kOutput, calls=%fused_computation.35 | convolution fusion | flops 3185786880 | bytes 9782432 | tf_op jit(solution)/shard_map/dot_general | solution.py:166
  70.8 44.1 %fusion.15 = f32[128,1440]{0,1:T(8,128)S(1)} fusion(f32[128,1440]{0,1:T(8,128)S(1)} %bitcast.222, f32[128,1440]{0,1:T(8,128)S(1)} %fusion.18, s32[1440]{0:T(1024)S(1)} %add_select_fusion.1, pred[1440]{0:T(1024)(128)(4,1)S(1)} %get-tuple-element.259, pred[128]{0:T(512)(128)(4,1)S(1)} %broadcast_compare_fusion.3), kind=kOutput, calls=%fused_computation.32 | convolution fusion | flops 3205969920 | bytes 2219168 | tf_op jit(solution)/shard_map/dot_general | solution.py:171
  114.9 12.8 %all_to_all.58 = f32[128,4,360]{0,2,1:T(8,128)S(1)} all-to-all(f32[128,4,360]{0,2,1:T(8,128)S(1)} %bitcast.228), channel_id=1, replica_groups=mesh['lon'=4,'lat'=8] {'lon'}, dimensions={1} | all-to-all | bytes 1474560 | tf_op jit(solution)/shard_map/all_to_all | solution.py:179
  128.1 5.9 %collective-permute-start = (f32[3,360,160]{1,2,0:T(8,128)S(1)}, f32[3,360,160]{1,2,0:T(8,128)S(1)}, u32[]{:S(2)}, u32[]{:S(2)}) collective-permute-start(f32[3,360,160]{1,2,0:T(8,128)S(1)} %get-tuple-element.191), channel_id=1, source_target_pairs={{0,1},{1,2},{2,3},{3,4},{4,5},{5,6},{6,7},{8,9},{9,10},{10,11},{11... | collective-permute-start | bytes 2073608 | tf_op jit(solution)/shard_map/ppermute | solution.py:28
  134.1 1.9 collective-permute-start.1
  136.0 0.6 compare_and_fusion.1
  136.6 5.7 %collective-permute-done = f32[3,360,160]{1,2,0:T(8,128)S(1)} collective-permute-done((f32[3,360,160]{1,2,0:T(8,128)S(1)}, f32[3,360,160]{1,2,0:T(8,128)S(1)}, u32[]{:S(2)}, u32[]{:S(2)}) %collective-permute-start) | collective-permute-done | bytes 691232 | tf_op jit(solution)/shard_map/ppermute | solution.py:28
  142.2 0.9 copy-done.7
  143.1 3.9 collective-permute-done.1
  146.9 1.5 fusion.12
  148.5 1.6 broadcast_in_dim.435
  150.1 2.9 reshape.8039
  153.0 2.7 multiply_multiply_fusion.6
  155.7 3.2 multiply_multiply_fusion.7
  159.0 0.6 fusion.23
  159.6 1.2 copy-done.2
  161.3 0.6 collective-permute-start.2
  161.9 1.2 slice_add_fusion.11
  163.1 23.5 %collective-permute-done.2 = f32[6,360,128]{2,1,0:T(8,128)} collective-permute-done((f32[6,360,128]{2,1,0:T(8,128)S(1)}, f32[6,360,128]{2,1,0:T(8,128)}, u32[]{:S(2)}, u32[]{:S(2)}) %collective-permute-start.2) | collective-permute-done | bytes 1105952 | tf_op jit(solution)/shard_map/ppermute | solution.py:18
  186.6 1.3 fusion.231
  188.7 0.6 copy-done.5
  190.0 2.1 collective-permute-start.4
  192.1 7.9 %collective-permute-done.3 = f32[4,3,160]{1,2,0:T(8,128)S(1)} collective-permute-done((f32[4,3,160]{1,2,0:T(8,128)S(1)}, f32[4,3,160]{1,2,0:T(8,128)S(1)}, u32[]{:S(2)}, u32[]{:S(2)}) %collective-permute-start.3) | collective-permute-done | bytes 7712 | tf_op jit(solution)/shard_map/ppermute | solution.py:28
  200.0 6.3 %collective-permute-done.4 = f32[4,3,160]{1,2,0:T(8,128)S(1)} collective-permute-done((f32[4,3,160]{1,2,0:T(8,128)S(1)}, f32[4,3,160]{1,2,0:T(8,128)S(1)}, u32[]{:S(2)}, u32[]{:S(2)}) %collective-permute-start.4) | collective-permute-done | bytes 7712 | tf_op jit(solution)/shard_map/ppermute | solution.py:29
  207.5 1.4 multiply_multiply_fusion.22
  210.6 1.3 fusion.38
  212.8 1.6 constant_dynamic-update-slice_fusion.63
  215.0 1.2 copy.48
  216.2 4.0 all-to-all-start.2
  220.2 38.1 %sine_select_fusion.21 = f32[1440,1440]{1,0:T(8,128)} fusion(s32[1440]{0:T(1024)S(1)} %copy-done.18, pred[1440]{0:T(1024)(128)(4,1)S(1)} %copy-done.94), kind=kLoop, calls=%fused_computation.3.clone.1.clone.clone.clone.clone.clone.1 | loop fusion | flops 20736000 | bytes 8301600 | tf_op jit(solution)/shard_map/dot_general | solution.py:166
  258.4 18.1 %fusion.17 = f32[128,1440]{0,1:T(8,128)S(1)} fusion(f32[128,1440]{0,1:T(8,128)S(1)} %bitcast.223, s32[1440]{0:T(1024)S(1)} %copy-done.18, f32[1440]{0:T(1024)S(1)} %copy-done.52, s32[128]{0:T(128)S(1)} %copy-done.98, pred[1440]{0:T(1024)(128)(4,1)S(1)} %copy-done.92, f32[1440,1440]{1,0:T(8,128)} %sine_select_fusion.21), kind=kOutput, calls=%fused_computation.34 | convolution fusion | flops 3185786880 | bytes 9782432 | tf_op jit(solution)/shard_map/dot_general | solution.py:166
  276.5 44.1 %fusion.16 = f32[128,1440]{0,1:T(8,128)S(1)} fusion(f32[128,1440]{0,1:T(8,128)S(1)} %bitcast.224, f32[128,1440]{0,1:T(8,128)S(1)} %fusion.17, s32[1440]{0:T(1024)S(1)} %copy-done.18, pred[1440]{0:T(1024)(128)(4,1)S(1)} %copy-done.94, pred[128]{0:T(512)(128)(4,1)S(1)} %copy-done.102), kind=kOutput, calls=%fused_computation.33 | convolution fusion | flops 3205969920 | bytes 2219168 | tf_op jit(solution)/shard_map/dot_general | solution.py:171
  320.6 12.7 %all_to_all.59 = f32[128,4,360]{0,2,1:T(8,128)S(1)} all-to-all(f32[128,4,360]{0,2,1:T(8,128)S(1)} %bitcast.227), channel_id=1, replica_groups=mesh['lon'=4,'lat'=8] {'lon'}, dimensions={1} | all-to-all | bytes 1474560 | tf_op jit(solution)/shard_map/all_to_all | solution.py:179
  333.7 5.9 %collective-permute-start.5 = (f32[3,360,160]{1,2,0:T(8,128)S(1)}, f32[3,360,160]{1,2,0:T(8,128)S(1)}, u32[]{:S(2)}, u32[]{:S(2)}) collective-permute-start(f32[3,360,160]{1,2,0:T(8,128)S(1)} %get-tuple-element.187), channel_id=1, source_target_pairs={{0,1},{1,2},{2,3},{3,4},{4,5},{5,6},{6,7},{8,9},{9,10},{10,11},{11... | collective-permute-start | bytes 2073608 | tf_op jit(solution)/shard_map/ppermute | solution.py:28
  339.5 1.9 collective-permute-start.6
  341.5 6.2 %collective-permute-done.5 = f32[3,360,160]{1,2,0:T(8,128)S(1)} collective-permute-done((f32[3,360,160]{1,2,0:T(8,128)S(1)}, f32[3,360,160]{1,2,0:T(8,128)S(1)}, u32[]{:S(2)}, u32[]{:S(2)}) %collective-permute-start.5) | collective-permute-done | bytes 691232 | tf_op jit(solution)/shard_map/ppermute | solution.py:28
  347.7 4.6 %collective-permute-done.6 = f32[3,360,160]{1,2,0:T(8,128)S(1)} collective-permute-done((f32[3,360,160]{1,2,0:T(8,128)S(1)}, f32[3,360,160]{1,2,0:T(8,128)S(1)}, u32[]{:S(2)}, u32[]{:S(2)}) %collective-permute-start.6) | collective-permute-done | bytes 691232 | tf_op jit(solution)/shard_map/ppermute | solution.py:29
  352.5 1.6 broadcast_in_dim.439
  354.2 2.9 reshape.8043
  357.1 2.7 multiply_multiply_fusion
  359.7 3.2 multiply_multiply_fusion.1
  363.0 0.6 fusion.28
  363.6 1.2 copy-done.3
  365.4 0.6 collective-permute-start.7
  365.9 1.2 slice_add_fusion.5
  367.1 23.5 %collective-permute-done.7 = f32[6,360,128]{2,1,0:T(8,128)S(1)} collective-permute-done((f32[6,360,128]{2,1,0:T(8,128)S(1)}, f32[6,360,128]{2,1,0:T(8,128)S(1)}, u32[]{:S(2)}, u32[]{:S(2)}) %collective-permute-start.7) | collective-permute-done | bytes 1105952 | tf_op jit(solution)/shard_map/ppermute | solution.py:18
  391.5 0.6 copy-done.6
  392.8 1.9 collective-permute-start.9
  394.7 8.0 %collective-permute-done.8 = f32[4,3,160]{1,2,0:T(8,128)S(1)} collective-permute-done((f32[4,3,160]{1,2,0:T(8,128)S(1)}, f32[4,3,160]{1,2,0:T(8,128)S(1)}, u32[]{:S(2)}, u32[]{:S(2)}) %collective-permute-start.8) | collective-permute-done | bytes 7712 | tf_op jit(solution)/shard_map/ppermute | solution.py:28
  402.7 6.3 %collective-permute-done.9 = f32[4,3,160]{1,2,0:T(8,128)S(1)} collective-permute-done((f32[4,3,160]{1,2,0:T(8,128)S(1)}, f32[4,3,160]{1,2,0:T(8,128)S(1)}, u32[]{:S(2)}, u32[]{:S(2)}) %collective-permute-start.9) | collective-permute-done | bytes 7712 | tf_op jit(solution)/shard_map/ppermute | solution.py:29
  410.2 1.4 multiply_multiply_fusion.16
  412.9 1.3 fusion.37
  414.2 1.1 copy.55
  (324 shorter events, 13.2 us)
Async XLA Ops:
  1.2 4.9 %copy-start.53 = (f32[4,360]{1,0:T(4,128)}, f32[4,360]{1,0:T(4,128)S(1)}, u32[]{:S(2)}) copy-start(f32[4,360]{1,0:T(4,128)S(1)} %get-tuple-element.243) | copy-start | bytes 17284
  1.2 4.9 %copy-start.55 = (f32[4,360]{1,0:T(4,128)}, f32[4,360]{1,0:T(4,128)S(1)}, u32[]{:S(2)}) copy-start(f32[4,360]{1,0:T(4,128)S(1)} %get-tuple-element.244) | copy-start | bytes 17284
  1.2 4.9 %copy-start.57 = (f32[4,360]{1,0:T(4,128)}, f32[4,360]{1,0:T(4,128)S(1)}, u32[]{:S(2)}) copy-start(f32[4,360]{1,0:T(4,128)S(1)} %get-tuple-element.245) | copy-start | bytes 17284
  1.2 4.9 %copy-start.59 = (f32[4,360]{1,0:T(4,128)}, f32[4,360]{1,0:T(4,128)S(1)}, u32[]{:S(2)}) copy-start(f32[4,360]{1,0:T(4,128)S(1)} %get-tuple-element.246) | copy-start | bytes 17284
  1.2 4.9 %copy-start.61 = (f32[4,360]{1,0:T(4,128)}, f32[4,360]{1,0:T(4,128)S(1)}, u32[]{:S(2)}) copy-start(f32[4,360]{1,0:T(4,128)S(1)} %get-tuple-element.247) | copy-start | bytes 17284
  1.2 4.9 %copy-start.63 = (f32[4,360]{1,0:T(4,128)}, f32[4,360]{1,0:T(4,128)S(1)}, u32[]{:S(2)}) copy-start(f32[4,360]{1,0:T(4,128)S(1)} %get-tuple-element.248) | copy-start | bytes 17284
  1.2 4.9 %copy-start.65 = (f32[4,360]{1,0:T(4,128)}, f32[4,360]{1,0:T(4,128)S(1)}, u32[]{:S(2)}) copy-start(f32[4,360]{1,0:T(4,128)S(1)} %get-tuple-element.249) | copy-start | bytes 17284
  1.2 4.9 %copy-start.67 = (f32[4,360]{1,0:T(4,128)}, f32[4,360]{1,0:T(4,128)S(1)}, u32[]{:S(2)}) copy-start(f32[4,360]{1,0:T(4,128)S(1)} %get-tuple-element.250) | copy-start | bytes 17284
  1.2 4.9 %copy-start.69 = (f32[4,360]{1,0:T(4,128)}, f32[4,360]{1,0:T(4,128)S(1)}, u32[]{:S(2)}) copy-start(f32[4,360]{1,0:T(4,128)S(1)} %get-tuple-element.251) | copy-start | bytes 17284
  1.3 4.9 %copy-start.71 = (f32[4,360]{1,0:T(4,128)}, f32[4,360]{1,0:T(4,128)S(1)}, u32[]{:S(2)}) copy-start(f32[4,360]{1,0:T(4,128)S(1)} %get-tuple-element.252) | copy-start | bytes 17284
  1.3 4.9 %copy-start.73 = (f32[4,360]{1,0:T(4,128)}, f32[4,360]{1,0:T(4,128)S(1)}, u32[]{:S(2)}) copy-start(f32[4,360]{1,0:T(4,128)S(1)} %get-tuple-element.253) | copy-start | bytes 17284
  1.3 4.9 %copy-start.75 = (f32[4,360]{1,0:T(4,128)}, f32[4,360]{1,0:T(4,128)S(1)}, u32[]{:S(2)}) copy-start(f32[4,360]{1,0:T(4,128)S(1)} %get-tuple-element.254) | copy-start | bytes 17284
  1.3 4.9 %copy-start.77 = (f32[4,360]{1,0:T(4,128)}, f32[4,360]{1,0:T(4,128)S(1)}, u32[]{:S(2)}) copy-start(f32[4,360]{1,0:T(4,128)S(1)} %get-tuple-element.255) | copy-start | bytes 17284
  1.3 4.9 %copy-start.79 = (f32[4,360]{1,0:T(4,128)}, f32[4,360]{1,0:T(4,128)S(1)}, u32[]{:S(2)}) copy-start(f32[4,360]{1,0:T(4,128)S(1)} %get-tuple-element.256) | copy-start | bytes 17284
  1.7 6.1 %copy-start.19 = (f32[1,4,360]{2,1,0:T(4,128)}, f32[1,4,360]{2,1,0:T(4,128)S(1)}, u32[]{:S(2)}) copy-start(f32[1,4,360]{2,1,0:T(4,128)S(1)} %get-tuple-element.127) | copy-start | bytes 17284
  1.7 6.1 %copy-start.21 = (f32[1,4,360]{2,1,0:T(4,128)}, f32[1,4,360]{2,1,0:T(4,128)S(1)}, u32[]{:S(2)}) copy-start(f32[1,4,360]{2,1,0:T(4,128)S(1)} %get-tuple-element.129) | copy-start | bytes 17284
  1.7 6.1 %copy-start.23 = (f32[1,4,360]{2,1,0:T(4,128)}, f32[1,4,360]{2,1,0:T(4,128)S(1)}, u32[]{:S(2)}) copy-start(f32[1,4,360]{2,1,0:T(4,128)S(1)} %get-tuple-element.131) | copy-start | bytes 17284
  1.7 6.1 %copy-start.25 = (f32[1,4,360]{2,1,0:T(4,128)}, f32[1,4,360]{2,1,0:T(4,128)S(1)}, u32[]{:S(2)}) copy-start(f32[1,4,360]{2,1,0:T(4,128)S(1)} %get-tuple-element.133) | copy-start | bytes 17284
  1.8 6.1 %copy-start.27 = (f32[1,4,360]{2,1,0:T(4,128)}, f32[1,4,360]{2,1,0:T(4,128)S(1)}, u32[]{:S(2)}) copy-start(f32[1,4,360]{2,1,0:T(4,128)S(1)} %get-tuple-element.135) | copy-start | bytes 17284
  1.8 6.1 %copy-start.29 = (f32[1,4,360]{2,1,0:T(4,128)}, f32[1,4,360]{2,1,0:T(4,128)S(1)}, u32[]{:S(2)}) copy-start(f32[1,4,360]{2,1,0:T(4,128)S(1)} %get-tuple-element.137) | copy-start | bytes 17284
  1.8 6.1 %copy-start.31 = (f32[1,4,360]{2,1,0:T(4,128)}, f32[1,4,360]{2,1,0:T(4,128)S(1)}, u32[]{:S(2)}) copy-start(f32[1,4,360]{2,1,0:T(4,128)S(1)} %get-tuple-element.139) | copy-start | bytes 17284
  1.8 6.1 %copy-start.33 = (f32[1,4,360]{2,1,0:T(4,128)}, f32[1,4,360]{2,1,0:T(4,128)S(1)}, u32[]{:S(2)}) copy-start(f32[1,4,360]{2,1,0:T(4,128)S(1)} %get-tuple-element.141) | copy-start | bytes 17284
  1.8 6.1 %copy-start.35 = (f32[1,4,360]{2,1,0:T(4,128)}, f32[1,4,360]{2,1,0:T(4,128)S(1)}, u32[]{:S(2)}) copy-start(f32[1,4,360]{2,1,0:T(4,128)S(1)} %get-tuple-element.143) | copy-start | bytes 17284
  1.8 6.1 %copy-start.37 = (f32[1,4,360]{2,1,0:T(4,128)}, f32[1,4,360]{2,1,0:T(4,128)S(1)}, u32[]{:S(2)}) copy-start(f32[1,4,360]{2,1,0:T(4,128)S(1)} %get-tuple-element.145) | copy-start | bytes 17284
  1.8 6.1 %copy-start.39 = (f32[1,4,360]{2,1,0:T(4,128)}, f32[1,4,360]{2,1,0:T(4,128)S(1)}, u32[]{:S(2)}) copy-start(f32[1,4,360]{2,1,0:T(4,128)S(1)} %get-tuple-element.147) | copy-start | bytes 17284
  1.8 6.1 %copy-start.41 = (f32[1,4,360]{2,1,0:T(4,128)}, f32[1,4,360]{2,1,0:T(4,128)S(1)}, u32[]{:S(2)}) copy-start(f32[1,4,360]{2,1,0:T(4,128)S(1)} %get-tuple-element.149) | copy-start | bytes 17284
  1.8 6.1 %copy-start.43 = (f32[1,4,360]{2,1,0:T(4,128)}, f32[1,4,360]{2,1,0:T(4,128)S(1)}, u32[]{:S(2)}) copy-start(f32[1,4,360]{2,1,0:T(4,128)S(1)} %get-tuple-element.151) | copy-start | bytes 17284
  1.8 6.1 %copy-start.45 = (f32[1,4,360]{2,1,0:T(4,128)}, f32[1,4,360]{2,1,0:T(4,128)S(1)}, u32[]{:S(2)}) copy-start(f32[1,4,360]{2,1,0:T(4,128)S(1)} %get-tuple-element.153) | copy-start | bytes 17284
  1.9 6.1 %copy-start.47 = (f32[1,4,360]{2,1,0:T(4,128)}, f32[1,4,360]{2,1,0:T(4,128)S(1)}, u32[]{:S(2)}) copy-start(f32[1,4,360]{2,1,0:T(4,128)S(1)} %get-tuple-element.155) | copy-start | bytes 17284
  1.9 6.1 %copy-start.49 = (f32[1,4,360]{2,1,0:T(4,128)}, f32[1,4,360]{2,1,0:T(4,128)S(1)}, u32[]{:S(2)}) copy-start(f32[1,4,360]{2,1,0:T(4,128)S(1)} %get-tuple-element.156) | copy-start | bytes 17284
  1.9 6.1 %copy-start.15 = (f32[1,4,360]{2,1,0:T(4,128)}, f32[1,4,360]{2,1,0:T(4,128)S(1)}, u32[]{:S(2)}) copy-start(f32[1,4,360]{2,1,0:T(4,128)S(1)} %get-tuple-element.154) | copy-start | bytes 17284
  1.9 6.2 %copy-start.13 = (f32[1,4,360]{2,1,0:T(4,128)}, f32[1,4,360]{2,1,0:T(4,128)S(1)}, u32[]{:S(2)}) copy-start(f32[1,4,360]{2,1,0:T(4,128)S(1)} %get-tuple-element.152) | copy-start | bytes 17284
  1.9 6.2 %copy-start.11 = (f32[1,4,360]{2,1,0:T(4,128)}, f32[1,4,360]{2,1,0:T(4,128)S(1)}, u32[]{:S(2)}) copy-start(f32[1,4,360]{2,1,0:T(4,128)S(1)} %get-tuple-element.150) | copy-start | bytes 17284
  1.9 6.3 %copy-start.9 = (f32[1,4,360]{2,1,0:T(4,128)}, f32[1,4,360]{2,1,0:T(4,128)S(1)}, u32[]{:S(2)}) copy-start(f32[1,4,360]{2,1,0:T(4,128)S(1)} %get-tuple-element.148) | copy-start | bytes 17284
  2.9 5.2 %copy-start.81 = (f32[4,360]{1,0:T(4,128)}, f32[4,360]{1,0:T(4,128)S(1)}, u32[]{:S(2)}) copy-start(f32[4,360]{1,0:T(4,128)S(1)} %get-tuple-element.223) | copy-start | bytes 17284
  2.9 5.2 %copy-start.83 = (f32[4,360]{1,0:T(4,128)}, f32[4,360]{1,0:T(4,128)S(1)}, u32[]{:S(2)}) copy-start(f32[4,360]{1,0:T(4,128)S(1)} %get-tuple-element.224) | copy-start | bytes 17284
  2.9 5.2 %copy-start.85 = (f32[4,360]{1,0:T(4,128)}, f32[4,360]{1,0:T(4,128)S(1)}, u32[]{:S(2)}) copy-start(f32[4,360]{1,0:T(4,128)S(1)} %get-tuple-element.230) | copy-start | bytes 17284
  2.9 5.2 %copy-start.87 = (f32[4,360]{1,0:T(4,128)}, f32[4,360]{1,0:T(4,128)S(1)}, u32[]{:S(2)}) copy-start(f32[4,360]{1,0:T(4,128)S(1)} %get-tuple-element.231) | copy-start | bytes 17284
  2.9 5.2 %copy-start.89 = (f32[4,360]{1,0:T(4,128)}, f32[4,360]{1,0:T(4,128)S(1)}, u32[]{:S(2)}) copy-start(f32[4,360]{1,0:T(4,128)S(1)} %get-tuple-element.232) | copy-start | bytes 17284
  9.9 42.3 %all-to-all-start = ((f32[4,128,360]{1,2,0:T(8,128)}), f32[4,128,360]{1,2,0:T(8,128)S(1)}, u32[]{:S(2)}, u32[]{:S(2)}) async-start(f32[4,128,360]{1,2,0:T(8,128)} %copy.40), calls=%async_computation | async-start | bytes 1474560 | tf_op jit(solution)/shard_map/all_to_all | solution.py:156
  13.8 57.0 %copy-start.17 = (s32[1440]{0:T(1024)}, s32[1440]{0:T(1024)S(1)}, u32[]{:S(2)}) copy-start(s32[1440]{0:T(1024)S(1)} %add_select_fusion.1) | copy-start | bytes 17284
  13.9 38.3 %copy-start.91 = (pred[1440]{0:T(1024)(128)(4,1)}, pred[1440]{0:T(1024)(128)(4,1)S(1)}, u32[]{:S(2)}) copy-start(pred[1440]{0:T(1024)(128)(4,1)S(1)} %get-tuple-element.260) | copy-start | bytes 4324
  13.9 56.9 %copy-start.93 = (pred[1440]{0:T(1024)(128)(4,1)}, pred[1440]{0:T(1024)(128)(4,1)S(1)}, u32[]{:S(2)}) copy-start(pred[1440]{0:T(1024)(128)(4,1)S(1)} %get-tuple-element.259) | copy-start | bytes 4324
  13.9 38.1 %copy-start.99 = (s32[4]{0:T(128)S(1)}, s32[4]{0:T(128)}, u32[]{:S(2)}) copy-start(s32[4]{0:T(128)} %param.19) | copy-start | bytes 52
  13.9 38.1 %copy-start.100 = (s32[4]{0:T(128)S(1)}, s32[4]{0:T(128)}, u32[]{:S(2)}) copy-start(s32[4]{0:T(128)} %param.18) | copy-start | bytes 52
  52.2 18.6 %copy-start.101 = (pred[128]{0:T(512)(128)(4,1)}, pred[128]{0:T(512)(128)(4,1)S(1)}, u32[]{:S(2)}) copy-start(pred[128]{0:T(512)(128)(4,1)S(1)} %broadcast_compare_fusion.3) | copy-start | bytes 388
  114.9 13.1 %copy-start.4 = (f32[4,360,32]{1,2,0:T(8,128)S(1)}, f32[4,360,32]{1,2,0:T(8,128)}, u32[]{:S(2)}) copy-start(f32[4,360,32]{1,2,0:T(8,128)} %param.16) | copy-start | bytes 552964
  128.1 14.1 %collective-permute-start = (f32[3,360,160]{1,2,0:T(8,128)S(1)}, f32[3,360,160]{1,2,0:T(8,128)S(1)}, u32[]{:S(2)}, u32[]{:S(2)}) collective-permute-start(f32[3,360,160]{1,2,0:T(8,128)S(1)} %get-tuple-element.191), channel_id=1, source_target_pairs={{0,1},{1,2},{2,3},{3,4},{4,5},{5,6},{6,7},{8,9},{9,10},{10,11},{11... | collective-permute-start | bytes 2073608 | tf_op jit(solution)/shard_map/ppermute | solution.py:28
  134.1 12.9 %collective-permute-start.1 = (f32[3,360,160]{1,2,0:T(8,128)S(1)}, f32[3,360,160]{1,2,0:T(8,128)}, u32[]{:S(2)}, u32[]{:S(2)}) collective-permute-start(f32[3,360,160]{1,2,0:T(8,128)S(1)} %get-tuple-element.192), channel_id=1, source_target_pairs={{1,0},{2,1},{3,2},{4,3},{5,4},{6,5},{7,6},{9,8},{10,9},{11,10},{12... | collective-permute-start | bytes 2073608 | tf_op jit(solution)/shard_map/ppermute | solution.py:29
  161.3 25.3 %collective-permute-start.2 = (f32[6,360,128]{2,1,0:T(8,128)S(1)}, f32[6,360,128]{2,1,0:T(8,128)}, u32[]{:S(2)}, u32[]{:S(2)}) collective-permute-start(f32[6,360,128]{2,1,0:T(8,128)S(1)} %copy.42), channel_id=1, source_target_pairs={{0,16},{16,0},{8,24},{24,8},{1,17},{17,1},{9,25},{25,9},{2,18},{18... | collective-permute-start | bytes 3317768 | tf_op jit(solution)/shard_map/ppermute | solution.py:18
  189.5 10.5 %collective-permute-start.3 = (f32[4,3,160]{1,2,0:T(8,128)S(1)}, f32[4,3,160]{1,2,0:T(8,128)S(1)}, u32[]{:S(2)}, u32[]{:S(2)}) collective-permute-start(f32[4,3,160]{1,2,0:T(8,128)S(1)} %get-tuple-element.189), channel_id=1, source_target_pairs={{0,8},{8,16},{16,24},{24,0},{1,9},{9,17},{17,25},{25,1},{2,10},{10... | collective-permute-start | bytes 23048 | tf_op jit(solution)/shard_map/ppermute | solution.py:28
  190.0 16.3 %collective-permute-start.4 = (f32[4,3,160]{1,2,0:T(8,128)S(1)}, f32[4,3,160]{1,2,0:T(8,128)S(1)}, u32[]{:S(2)}, u32[]{:S(2)}) collective-permute-start(f32[4,3,160]{1,2,0:T(8,128)S(1)} %get-tuple-element.190), channel_id=1, source_target_pairs={{8,0},{16,8},{24,16},{0,24},{9,1},{17,9},{25,17},{1,25},{10,2},{18... | collective-permute-start | bytes 23048 | tf_op jit(solution)/shard_map/ppermute | solution.py:29
  214.9 5.3 %copy-start.18 = (s32[1440]{0:T(1024)S(1)}, s32[1440]{0:T(1024)}, u32[]{:S(2)}) copy-start(s32[1440]{0:T(1024)} %copy-done.17) | copy-start | bytes 17284
  214.9 5.3 %copy-start.94 = (pred[1440]{0:T(1024)(128)(4,1)S(1)}, pred[1440]{0:T(1024)(128)(4,1)}, u32[]{:S(2)}) copy-start(pred[1440]{0:T(1024)(128)(4,1)} %copy-done.93) | copy-start | bytes 4324
  216.2 42.1 %all-to-all-start.2 = ((f32[4,128,360]{1,2,0:T(8,128)}), f32[4,128,360]{1,2,0:T(8,128)S(1)}, u32[]{:S(2)}, u32[]{:S(2)}) async-start(f32[4,128,360]{1,2,0:T(8,128)} %copy.48), calls=%async_computation.2 | async-start | bytes 1474560 | tf_op jit(solution)/shard_map/all_to_all | solution.py:156
  220.2 38.1 %copy-start.52 = (f32[1440]{0:T(1024)S(1)}, f32[1440]{0:T(1024)}, u32[]{:S(2)}) copy-start(f32[1440]{0:T(1024)} %copy-done.51) | copy-start | bytes 17284
  220.2 38.1 %copy-start.92 = (pred[1440]{0:T(1024)(128)(4,1)S(1)}, pred[1440]{0:T(1024)(128)(4,1)}, u32[]{:S(2)}) copy-start(pred[1440]{0:T(1024)(128)(4,1)} %copy-done.91) | copy-start | bytes 4324
  220.2 38.1 %copy-start.98 = (s32[128]{0:T(128)S(1)}, s32[128]{0:T(128)}, u32[]{:S(2)}) copy-start(s32[128]{0:T(128)} %copy-done.97) | copy-start | bytes 1540
  258.3 18.1 %copy-start.102 = (pred[128]{0:T(512)(128)(4,1)S(1)}, pred[128]{0:T(512)(128)(4,1)}, u32[]{:S(2)}) copy-start(pred[128]{0:T(512)(128)(4,1)} %copy-done.101) | copy-start | bytes 388
  333.7 14.0 %collective-permute-start.5 = (f32[3,360,160]{1,2,0:T(8,128)S(1)}, f32[3,360,160]{1,2,0:T(8,128)S(1)}, u32[]{:S(2)}, u32[]{:S(2)}) collective-permute-start(f32[3,360,160]{1,2,0:T(8,128)S(1)} %get-tuple-element.187), channel_id=1, source_target_pairs={{0,1},{1,2},{2,3},{3,4},{4,5},{5,6},{6,7},{8,9},{9,10},{10,11},{11... | collective-permute-start | bytes 2073608 | tf_op jit(solution)/shard_map/ppermute | solution.py:28
  339.5 12.8 %collective-permute-start.6 = (f32[3,360,160]{1,2,0:T(8,128)S(1)}, f32[3,360,160]{1,2,0:T(8,128)S(1)}, u32[]{:S(2)}, u32[]{:S(2)}) collective-permute-start(f32[3,360,160]{1,2,0:T(8,128)S(1)} %get-tuple-element.188), channel_id=1, source_target_pairs={{1,0},{2,1},{3,2},{4,3},{5,4},{6,5},{7,6},{9,8},{10,9},{11,10},{12... | collective-permute-start | bytes 2073608 | tf_op jit(solution)/shard_map/ppermute | solution.py:29
  365.4 25.3 %collective-permute-start.7 = (f32[6,360,128]{2,1,0:T(8,128)S(1)}, f32[6,360,128]{2,1,0:T(8,128)S(1)}, u32[]{:S(2)}, u32[]{:S(2)}) collective-permute-start(f32[6,360,128]{2,1,0:T(8,128)S(1)} %copy.50), channel_id=1, source_target_pairs={{0,16},{16,0},{8,24},{24,8},{1,17},{17,1},{9,25},{25,9},{2,18},{18... | collective-permute-start | bytes 3317768 | tf_op jit(solution)/shard_map/ppermute | solution.py:18
  392.3 10.4 %collective-permute-start.8 = (f32[4,3,160]{1,2,0:T(8,128)S(1)}, f32[4,3,160]{1,2,0:T(8,128)S(1)}, u32[]{:S(2)}, u32[]{:S(2)}) collective-permute-start(f32[4,3,160]{1,2,0:T(8,128)S(1)} %get-tuple-element.185), channel_id=1, source_target_pairs={{0,8},{8,16},{16,24},{24,0},{1,9},{9,17},{17,25},{25,1},{2,10},{10... | collective-permute-start | bytes 23048 | tf_op jit(solution)/shard_map/ppermute | solution.py:28
  392.8 16.2 %collective-permute-start.9 = (f32[4,3,160]{1,2,0:T(8,128)S(1)}, f32[4,3,160]{1,2,0:T(8,128)S(1)}, u32[]{:S(2)}, u32[]{:S(2)}) collective-permute-start(f32[4,3,160]{1,2,0:T(8,128)S(1)} %get-tuple-element.186), channel_id=1, source_target_pairs={{8,0},{16,8},{24,16},{0,24},{9,1},{17,9},{25,17},{1,25},{10,2},{18... | collective-permute-start | bytes 23048 | tf_op jit(solution)/shard_map/ppermute | solution.py:29
  (51 other events, 105.6 us)
where the time goes:
time: 419 us; the launch traced here: 416 us
  matrix products  124 us (30%)
  other arithmetic  110 us (26%)
  waiting for transfers between devices  95.9 us (23%)
  starting transfers between devices  29.8 us (7%)
  local copies, waits for them, and re-layouts  27.4 us (7%)
  blocking collectives  25.5 us (6%)
    dot_general x2, matrix products, filter_rows(): lax.dot_general(weighted, table, (((1,), (1,)), ((), ())), precision=lax....  88.2 us
    dot_general x2, other arithmetic, filter_rows(): jnp.dot(circles, table, precision=lax.Precision.HIGHEST, preferred_elemen...  76.2 us
    ppermute x2, waiting for transfers between devices, partner(): return lax.ppermute(block, axis, route)  47 us
    dot_general x2, matrix products, filter_rows(): jnp.dot(circles, table, precision=lax.Precision.HIGHEST, preferred_elemen...  36.1 us
    ppermute x4, waiting for transfers between devices, padded_2(): before = lax.ppermute(last, axis, up)  27.7 us
    all_to_all x2, blocking collectives, filter_rows(): return lax.all_to_all(mixed, 'lon', split_axis=1, concat_axis=0, tiled=True)  25.5 us
    ppermute x4, waiting for transfers between devices, padded_2(): after = lax.ppermute(initial, axis, down)  21.1 us
    mul x8, other arithmetic, spread_flux(): term = jnp.pad(weights[position] * jump, padding)  15.4 us
  transfers between devices with their start and end apart: 12, of which 10 were waited for; matrix products, arithmetic and copies ran while one was open for 19% of the time, Pallas kernels for 0%

commit v1 on v0

--- a/solution.py
+++ b/solution.py
@@ -4,6 +4,7 @@
 import jax.numpy as jnp
 from jax import lax
 from jax.sharding import PartitionSpec as P
+from jax.lax import all_to_all, psum
 
 SUBSTEPS = 2
 
@@ -176,7 +177,10 @@
         preferred_element_type=jnp.float32,
     )
     mixed = jnp.where((row_flag > 0)[:, None], smooth, circles)
-    return lax.all_to_all(mixed, "lon", split_axis=1, concat_axis=0, tiled=True)
+    links_link = lambda t0: jnp.concatenate(
+        all_to_all(jnp.stack(jnp.split(t0, psum(1, "lon"), 1)), "lon", 0, 0), 0
+    )
+    return links_link(mixed)
 
 
 def widen(courant, tracers):

time: 419 us -> 430 us (1.026)
  local copies, waits for them, and re-layouts: 27.4 us -> 58.9 us
  waiting for transfers between devices: 95.9 us -> 77.8 us
  blocking collectives: 25.5 us -> 12.8 us
  other arithmetic: 110 us -> 116 us
    ppermute x4, waiting for transfers between devices: 27.7 us -> 11 us  [padded_2(): before = lax.ppermute(last, axis, up)]
    all_to_all x2 -> x1, blocking collectives: 25.5 us -> 12.8 us  [filter_rows(): all_to_all(jnp.stack(jnp.split(t0, psum(1, 'lon'), 1)), 'lon', 0, 0)]
    slice x0 -> x6, local copies, waits for them, and re-layouts: none -> 12.6 us  [the longest x2 5.77 us: spread_flux(): lax.slice_in_dim(courant_ext, 0, length - 1, axis=axis_dim)]
    ppermute x4, waiting for transfers between devices: 21.1 us -> 9.83 us  [padded_2(): after = lax.ppermute(initial, axis, down)]
    all_to_all x0 -> x1, waiting for transfers between devices: none -> 9.48 us  [filter_rows(): all_to_all(jnp.stack(jnp.split(t0, psum(1, 'lon'), 1)), 'lon', 0, 0)]
    ppermute x0 -> x4, local copies, waits for them, and re-layouts: none -> 8.9 us  [the longest x2 4.95 us: padded_2(): after = lax.ppermute(initial, axis, down)]
    unnamed x241 -> x179, local copies, waits for them, and re-layouts: 7.07 us -> 15.6 us
  transfers between devices with their start and end apart: 12 -> 13, of which waited for: 10 -> 10; matrix products, arithmetic and copies ran while one was open for 19% -> 20% of each run, Pallas kernels for 0% -> 0%
where the time goes in v1:
time: 430 us; the launch traced here: 425 us
  matrix products  124 us (29%)
  other arithmetic  116 us (27%)
  waiting for transfers between devices  77.8 us (18%)
  local copies, waits for them, and re-layouts  58.9 us (14%)
  starting transfers between devices  32.4 us (8%)
  blocking collectives  12.8 us (3%)
    dot_general x2, matrix products, filter_rows(): lax.dot_general(weighted, table, (((1,), (1,)), ((), ())), precision=lax....  88.2 us
    dot_general x2, other arithmetic, filter_rows(): jnp.dot(circles, table, precision=lax.Precision.HIGHEST, preferred_elemen...  76.1 us
    ppermute x2, waiting for transfers between devices, partner(): return lax.ppermute(block, axis, route)  47.5 us
    dot_general x2, matrix products, filter_rows(): jnp.dot(circles, table, precision=lax.Precision.HIGHEST, preferred_elemen...  36.2 us
    mul x8, other arithmetic, spread_flux(): term = jnp.pad(weights[position] * jump, padding)  16.7 us
    unnamed x179, local copies, waits for them, and re-layouts  15.6 us
    all_to_all x1, blocking collectives, filter_rows(): all_to_all(jnp.stack(jnp.split(t0, psum(1, 'lon'), 1)), 'lon', 0, 0)  12.8 us
    ppermute x4, starting transfers between devices, padded_2(): before = lax.ppermute(last, axis, up)  12.1 us
  transfers between devices with their start and end apart: 13, of which 10 were waited for; matrix products, arithmetic and copies ran while one was open for 20% of the time, Pallas kernels for 0%

profile of v1, /device:TPU:9, one launch (start us, length us, event | category | flops | bytes accessed | tf_op | source)
XLA Modules:
  0.0 424.9 jit_solution(7688263944289875673)
XLA Ops:
  6.2 1.6 constant_dynamic-update-slice_fusion.31
  9.8 4.0 all-to-all-start
  13.9 38.1 %sine_select_fusion.22 = f32[1440,1440]{1,0:T(8,128)} fusion(s32[1440]{0:T(1024)S(1)} %add_select_fusion.1, pred[1440]{0:T(1024)(128)(4,1)S(1)} %get-tuple-element.271), kind=kLoop, calls=%fused_computation.3.clone.3.clone.clone.clone.clone.clone | loop fusion | flops 20736000 | bytes 8301600 | tf_op jit(solution)/shard_map/dot_general | solution.py:167
  52.2 18.1 %fusion.18 = f32[128,1440]{0,1:T(8,128)S(1)} fusion(f32[128,1440]{0,1:T(8,128)S(1)} %bitcast.233, s32[1440]{0:T(1024)S(1)} %add_select_fusion.1, f32[1440]{0:T(1024)S(1)} %select_multiply_fusion, s32[128]{0:T(128)S(1)} %get-tuple-element.54, pred[1440]{0:T(1024)(128)(4,1)S(1)} %get-tuple-element.272, f32[1440,1440]{1,0:T(8,128)} %sine_select_fusion.22), kind=kOutput, calls=%fused_computation.35 | convolution fusion | flops 3185786880 | bytes 9782432 | tf_op jit(solution)/shard_map/dot_general | solution.py:167
  70.3 44.1 %fusion.15 = f32[128,1440]{0,1:T(8,128)S(1)} fusion(f32[128,1440]{0,1:T(8,128)S(1)} %bitcast.234, f32[128,1440]{0,1:T(8,128)S(1)} %fusion.18, s32[1440]{0:T(1024)S(1)} %add_select_fusion.1, pred[1440]{0:T(1024)(128)(4,1)S(1)} %get-tuple-element.271, pred[128]{0:T(512)(128)(4,1)S(1)} %broadcast_compare_fusion.3), kind=kOutput, calls=%fused_computation.32 | convolution fusion | flops 3205969920 | bytes 2219168 | tf_op jit(solution)/shard_map/dot_general | solution.py:172
  115.4 3.8 all-to-all-start.1
  119.5 9.5 %all-to-all-done.1 = f32[4,128,360]{1,2,0:T(8,128)S(1)} async-done(((f32[4,128,360]{1,2,0:T(8,128)}), f32[4,128,360]{1,2,0:T(8,128)S(1)}, u32[]{:S(2)}, u32[]{:S(2)}) %all-to-all-start.1) | async-done | bytes 737312 | tf_op jit(solution)/shard_map/all_to_all | solution.py:181
  129.0 1.2 fusion.38
  130.2 1.6 copy.54
  131.8 4.6 %collective-permute-start = (f32[3,360,160]{1,2,0:T(8,128)S(1)}, f32[3,360,160]{1,2,0:T(8,128)}, u32[]{:S(2)}, u32[]{:S(2)}) collective-permute-start(f32[3,360,160]{1,2,0:T(8,128)S(1)} %copy.54), channel_id=1, source_target_pairs={{0,1},{1,2},{2,3},{3,4},{4,5},{5,6},{6,7},{8,9},{9,10},{10,11},{11... | collective-permute-start | bytes 2073608 | tf_op jit(solution)/shard_map/ppermute | solution.py:29
  136.4 1.2 copy.55
  137.6 1.9 collective-permute-start.1
  140.0 4.7 %collective-permute-done = f32[3,360,160]{1,2,0:T(8,128)} collective-permute-done((f32[3,360,160]{1,2,0:T(8,128)S(1)}, f32[3,360,160]{1,2,0:T(8,128)}, u32[]{:S(2)}, u32[]{:S(2)}) %collective-permute-start) | collective-permute-done | bytes 691232 | tf_op jit(solution)/shard_map/ppermute | solution.py:29
  144.8 1.5 copy.56
  146.2 4.4 %collective-permute-done.1 = f32[3,360,160]{1,2,0:T(8,128)} collective-permute-done((f32[3,360,160]{1,2,0:T(8,128)}, f32[3,360,160]{1,2,0:T(8,128)}, u32[]{:S(2)}, u32[]{:S(2)}) %collective-permute-start.1) | collective-permute-done | bytes 691232 | tf_op jit(solution)/shard_map/ppermute | solution.py:30
  150.7 2.5 copy.57
  153.2 1.5 fusion.10
  154.7 1.8 copy-done.1
  157.5 2.0 reshape.8029
  159.5 2.9 slice.1682
  162.4 2.4 copy.77
  164.8 2.9 multiply_multiply_fusion.6
  167.7 3.0 multiply_multiply_fusion.7
  173.0 1.2 collective-permute-start.2
  174.4 1.2 slice_add_fusion.11
  175.6 22.9 %collective-permute-done.2 = f32[6,360,128]{2,1,0:T(8,128)} collective-permute-done((f32[6,360,128]{2,1,0:T(8,128)}, f32[6,360,128]{2,1,0:T(8,128)}, u32[]{:S(2)}, u32[]{:S(2)}) %collective-permute-start.2) | collective-permute-done | bytes 1105952 | tf_op jit(solution)/shard_map/ppermute | solution.py:19
  198.5 1.3 fusion.231
  201.9 1.2 collective-permute-start.4
  207.5 1.4 copy.75
  208.9 1.8 multiply_multiply_fusion.23
  210.7 1.3 multiply_multiply_fusion.22
  212.4 1.3 fusion.40
  213.8 1.4 copy.63
  215.3 1.8 constant_dynamic-update-slice_fusion.63
  218.5 2.3 copy.64
  220.8 3.9 all-to-all-start.2
  224.8 38.1 %sine_select_fusion.21 = f32[1440,1440]{1,0:T(8,128)} fusion(s32[1440]{0:T(1024)S(1)} %copy-done.17, pred[1440]{0:T(1024)(128)(4,1)S(1)} %copy-done.63), kind=kLoop, calls=%fused_computation.3.clone.1.clone.clone.clone.clone.clone.1 | loop fusion | flops 20736000 | bytes 8301600 | tf_op jit(solution)/shard_map/dot_general | solution.py:167
  262.8 18.1 %fusion.17 = f32[128,1440]{0,1:T(8,128)S(1)} fusion(f32[128,1440]{0,1:T(8,128)S(1)} %bitcast.235, s32[1440]{0:T(1024)S(1)} %copy-done.17, f32[1440]{0:T(1024)S(1)} %copy-done.38, s32[128]{0:T(128)S(1)} %copy-done.66, pred[1440]{0:T(1024)(128)(4,1)S(1)} %copy-done.61, f32[1440,1440]{1,0:T(8,128)} %sine_select_fusion.21), kind=kOutput, calls=%fused_computation.34 | convolution fusion | flops 3185786880 | bytes 9782432 | tf_op jit(solution)/shard_map/dot_general | solution.py:167
  281.0 44.1 %fusion.16 = f32[128,1440]{0,1:T(8,128)S(1)} fusion(f32[128,1440]{0,1:T(8,128)S(1)} %bitcast.236, f32[128,1440]{0,1:T(8,128)S(1)} %fusion.17, s32[1440]{0:T(1024)S(1)} %copy-done.17, pred[1440]{0:T(1024)(128)(4,1)S(1)} %copy-done.63, pred[128]{0:T(512)(128)(4,1)S(1)} %copy-done.70), kind=kOutput, calls=%fused_computation.33 | convolution fusion | flops 3205969920 | bytes 2219168 | tf_op jit(solution)/shard_map/dot_general | solution.py:172
  325.2 12.8 %all_to_all.42 = f32[4,128,360]{1,2,0:T(8,128)S(1)} all-to-all(f32[4,128,360]{1,2,0:T(8,128)S(1)} %pad_maximum_fusion.9), channel_id=1, replica_groups=mesh['lon'=4,'lat'=8] {'lon'}, dimensions={0} | all-to-all | bytes 1474560 | tf_op jit(solution)/shard_map/all_to_all | solution.py:181
  338.0 1.5 fusion.37
  339.5 1.6 copy.66
  341.1 5.8 %collective-permute-start.5 = (f32[3,360,160]{1,2,0:T(8,128)S(1)}, f32[3,360,160]{1,2,0:T(8,128)}, u32[]{:S(2)}, u32[]{:S(2)}) collective-permute-start(f32[3,360,160]{1,2,0:T(8,128)S(1)} %copy.66), channel_id=1, source_target_pairs={{0,1},{1,2},{2,3},{3,4},{4,5},{5,6},{6,7},{8,9},{9,10},{10,11},{11... | collective-permute-start | bytes 2073608 | tf_op jit(solution)/shard_map/ppermute | solution.py:29
  346.9 2.5 copy.67
  349.4 1.9 collective-permute-start.6
  351.3 4.0 collective-permute-done.5
  355.3 2.5 copy.68
  357.8 4.7 %collective-permute-done.6 = f32[3,360,160]{1,2,0:T(8,128)} collective-permute-done((f32[3,360,160]{1,2,0:T(8,128)}, f32[3,360,160]{1,2,0:T(8,128)}, u32[]{:S(2)}, u32[]{:S(2)}) %collective-permute-start.6) | collective-permute-done | bytes 691232 | tf_op jit(solution)/shard_map/ppermute | solution.py:30
  362.4 2.5 copy.69
  364.9 1.8 fusion.12
  366.8 1.8 copy-done
  368.6 1.4 slice.1738
  370.0 2.0 copy.70
  372.0 1.7 broadcast_in_dim.439
  373.7 2.9 reshape.8033
  376.6 2.9 slice.1740
  379.5 2.4 copy.78
  381.9 2.9 multiply_multiply_fusion
  384.9 3.0 multiply_multiply_fusion.1
  389.4 24.6 %collective-permute-done.7 = f32[6,360,128]{2,1,0:T(8,128)S(1)} collective-permute-done((f32[6,360,128]{2,1,0:T(8,128)S(1)}, f32[6,360,128]{2,1,0:T(8,128)S(1)}, u32[]{:S(2)}, u32[]{:S(2)}) %collective-permute-start.7) | collective-permute-done | bytes 1105952 | tf_op jit(solution)/shard_map/ppermute | solution.py:19
  415.4 1.9 collective-permute-start.9
  419.8 1.4 copy.76
  421.6 1.3 multiply_multiply_fusion.16
  423.3 1.3 fusion.39
  (274 shorter events, 27.2 us)
Async XLA Ops:
  1.2 4.9 %copy-start.41 = (f32[4,360]{1,0:T(4,128)}, f32[4,360]{1,0:T(4,128)S(1)}, u32[]{:S(2)}) copy-start(f32[4,360]{1,0:T(4,128)S(1)} %get-tuple-element.255) | copy-start | bytes 17284
  1.2 4.9 %copy-start.42 = (f32[4,360]{1,0:T(4,128)}, f32[4,360]{1,0:T(4,128)S(1)}, u32[]{:S(2)}) copy-start(f32[4,360]{1,0:T(4,128)S(1)} %get-tuple-element.256) | copy-start | bytes 17284
  1.2 4.9 %copy-start.43 = (f32[4,360]{1,0:T(4,128)}, f32[4,360]{1,0:T(4,128)S(1)}, u32[]{:S(2)}) copy-start(f32[4,360]{1,0:T(4,128)S(1)} %get-tuple-element.257) | copy-start | bytes 17284
  1.2 4.9 %copy-start.44 = (f32[4,360]{1,0:T(4,128)}, f32[4,360]{1,0:T(4,128)S(1)}, u32[]{:S(2)}) copy-start(f32[4,360]{1,0:T(4,128)S(1)} %get-tuple-element.258) | copy-start | bytes 17284
  1.2 4.9 %copy-start.45 = (f32[4,360]{1,0:T(4,128)}, f32[4,360]{1,0:T(4,128)S(1)}, u32[]{:S(2)}) copy-start(f32[4,360]{1,0:T(4,128)S(1)} %get-tuple-element.259) | copy-start | bytes 17284
  1.2 4.9 %copy-start.46 = (f32[4,360]{1,0:T(4,128)}, f32[4,360]{1,0:T(4,128)S(1)}, u32[]{:S(2)}) copy-start(f32[4,360]{1,0:T(4,128)S(1)} %get-tuple-element.260) | copy-start | bytes 17284
  1.2 4.9 %copy-start.47 = (f32[4,360]{1,0:T(4,128)}, f32[4,360]{1,0:T(4,128)S(1)}, u32[]{:S(2)}) copy-start(f32[4,360]{1,0:T(4,128)S(1)} %get-tuple-element.261) | copy-start | bytes 17284
  1.2 4.9 %copy-start.48 = (f32[4,360]{1,0:T(4,128)}, f32[4,360]{1,0:T(4,128)S(1)}, u32[]{:S(2)}) copy-start(f32[4,360]{1,0:T(4,128)S(1)} %get-tuple-element.262) | copy-start | bytes 17284
  1.2 4.9 %copy-start.49 = (f32[4,360]{1,0:T(4,128)}, f32[4,360]{1,0:T(4,128)S(1)}, u32[]{:S(2)}) copy-start(f32[4,360]{1,0:T(4,128)S(1)} %get-tuple-element.263) | copy-start | bytes 17284
  1.3 4.9 %copy-start.50 = (f32[4,360]{1,0:T(4,128)}, f32[4,360]{1,0:T(4,128)S(1)}, u32[]{:S(2)}) copy-start(f32[4,360]{1,0:T(4,128)S(1)} %get-tuple-element.264) | copy-start | bytes 17284
  1.3 4.9 %copy-start.51 = (f32[4,360]{1,0:T(4,128)}, f32[4,360]{1,0:T(4,128)S(1)}, u32[]{:S(2)}) copy-start(f32[4,360]{1,0:T(4,128)S(1)} %get-tuple-element.265) | copy-start | bytes 17284
  1.7 6.1 %copy-start.20 = (f32[1,4,360]{2,1,0:T(4,128)}, f32[1,4,360]{2,1,0:T(4,128)S(1)}, u32[]{:S(2)}) copy-start(f32[1,4,360]{2,1,0:T(4,128)S(1)} %get-tuple-element.131) | copy-start | bytes 17284
  1.7 6.1 %copy-start.22 = (f32[1,4,360]{2,1,0:T(4,128)}, f32[1,4,360]{2,1,0:T(4,128)S(1)}, u32[]{:S(2)}) copy-start(f32[1,4,360]{2,1,0:T(4,128)S(1)} %get-tuple-element.133) | copy-start | bytes 17284
  1.7 6.1 %copy-start.23 = (f32[1,4,360]{2,1,0:T(4,128)}, f32[1,4,360]{2,1,0:T(4,128)S(1)}, u32[]{:S(2)}) copy-start(f32[1,4,360]{2,1,0:T(4,128)S(1)} %get-tuple-element.135) | copy-start | bytes 17284
  1.7 6.1 %copy-start.24 = (f32[1,4,360]{2,1,0:T(4,128)}, f32[1,4,360]{2,1,0:T(4,128)S(1)}, u32[]{:S(2)}) copy-start(f32[1,4,360]{2,1,0:T(4,128)S(1)} %get-tuple-element.137) | copy-start | bytes 17284
  1.8 6.1 %copy-start.25 = (f32[1,4,360]{2,1,0:T(4,128)}, f32[1,4,360]{2,1,0:T(4,128)S(1)}, u32[]{:S(2)}) copy-start(f32[1,4,360]{2,1,0:T(4,128)S(1)} %get-tuple-element.139) | copy-start | bytes 17284
  1.8 6.1 %copy-start.26 = (f32[1,4,360]{2,1,0:T(4,128)}, f32[1,4,360]{2,1,0:T(4,128)S(1)}, u32[]{:S(2)}) copy-start(f32[1,4,360]{2,1,0:T(4,128)S(1)} %get-tuple-element.141) | copy-start | bytes 17284
  1.8 6.1 %copy-start.27 = (f32[1,4,360]{2,1,0:T(4,128)}, f32[1,4,360]{2,1,0:T(4,128)S(1)}, u32[]{:S(2)}) copy-start(f32[1,4,360]{2,1,0:T(4,128)S(1)} %get-tuple-element.143) | copy-start | bytes 17284
  1.8 6.1 %copy-start.28 = (f32[1,4,360]{2,1,0:T(4,128)}, f32[1,4,360]{2,1,0:T(4,128)S(1)}, u32[]{:S(2)}) copy-start(f32[1,4,360]{2,1,0:T(4,128)S(1)} %get-tuple-element.145) | copy-start | bytes 17284
  1.8 6.1 %copy-start.29 = (f32[1,4,360]{2,1,0:T(4,128)}, f32[1,4,360]{2,1,0:T(4,128)S(1)}, u32[]{:S(2)}) copy-start(f32[1,4,360]{2,1,0:T(4,128)S(1)} %get-tuple-element.147) | copy-start | bytes 17284
  1.8 6.1 %copy-start.30 = (f32[1,4,360]{2,1,0:T(4,128)}, f32[1,4,360]{2,1,0:T(4,128)S(1)}, u32[]{:S(2)}) copy-start(f32[1,4,360]{2,1,0:T(4,128)S(1)} %get-tuple-element.149) | copy-start | bytes 17284
  1.8 6.1 %copy-start.31 = (f32[1,4,360]{2,1,0:T(4,128)}, f32[1,4,360]{2,1,0:T(4,128)S(1)}, u32[]{:S(2)}) copy-start(f32[1,4,360]{2,1,0:T(4,128)S(1)} %get-tuple-element.151) | copy-start | bytes 17284
  1.8 6.1 %copy-start.32 = (f32[1,4,360]{2,1,0:T(4,128)}, f32[1,4,360]{2,1,0:T(4,128)S(1)}, u32[]{:S(2)}) copy-start(f32[1,4,360]{2,1,0:T(4,128)S(1)} %get-tuple-element.153) | copy-start | bytes 17284
  1.8 6.1 %copy-start.33 = (f32[1,4,360]{2,1,0:T(4,128)}, f32[1,4,360]{2,1,0:T(4,128)S(1)}, u32[]{:S(2)}) copy-start(f32[1,4,360]{2,1,0:T(4,128)S(1)} %get-tuple-element.155) | copy-start | bytes 17284
  1.8 6.1 %copy-start.34 = (f32[1,4,360]{2,1,0:T(4,128)}, f32[1,4,360]{2,1,0:T(4,128)S(1)}, u32[]{:S(2)}) copy-start(f32[1,4,360]{2,1,0:T(4,128)S(1)} %get-tuple-element.157) | copy-start | bytes 17284
  1.9 6.1 %copy-start.35 = (f32[1,4,360]{2,1,0:T(4,128)}, f32[1,4,360]{2,1,0:T(4,128)S(1)}, u32[]{:S(2)}) copy-start(f32[1,4,360]{2,1,0:T(4,128)S(1)} %get-tuple-element.159) | copy-start | bytes 17284
  1.9 6.1 %copy-start.36 = (f32[1,4,360]{2,1,0:T(4,128)}, f32[1,4,360]{2,1,0:T(4,128)S(1)}, u32[]{:S(2)}) copy-start(f32[1,4,360]{2,1,0:T(4,128)S(1)} %get-tuple-element.160) | copy-start | bytes 17284
  1.9 6.1 %copy-start.14 = (f32[1,4,360]{2,1,0:T(4,128)}, f32[1,4,360]{2,1,0:T(4,128)S(1)}, u32[]{:S(2)}) copy-start(f32[1,4,360]{2,1,0:T(4,128)S(1)} %get-tuple-element.158) | copy-start | bytes 17284
  1.9 6.2 %copy-start.12 = (f32[1,4,360]{2,1,0:T(4,128)}, f32[1,4,360]{2,1,0:T(4,128)S(1)}, u32[]{:S(2)}) copy-start(f32[1,4,360]{2,1,0:T(4,128)S(1)} %get-tuple-element.156) | copy-start | bytes 17284
  1.9 6.2 %copy-start.10 = (f32[1,4,360]{2,1,0:T(4,128)}, f32[1,4,360]{2,1,0:T(4,128)S(1)}, u32[]{:S(2)}) copy-start(f32[1,4,360]{2,1,0:T(4,128)S(1)} %get-tuple-element.154) | copy-start | bytes 17284
  1.9 6.3 %copy-start.8 = (f32[1,4,360]{2,1,0:T(4,128)}, f32[1,4,360]{2,1,0:T(4,128)S(1)}, u32[]{:S(2)}) copy-start(f32[1,4,360]{2,1,0:T(4,128)S(1)} %get-tuple-element.152) | copy-start | bytes 17284
  2.9 5.1 %copy-start.55 = (f32[4,360]{1,0:T(4,128)}, f32[4,360]{1,0:T(4,128)S(1)}, u32[]{:S(2)}) copy-start(f32[4,360]{1,0:T(4,128)S(1)} %get-tuple-element.235) | copy-start | bytes 17284
  2.9 5.1 %copy-start.56 = (f32[4,360]{1,0:T(4,128)}, f32[4,360]{1,0:T(4,128)S(1)}, u32[]{:S(2)}) copy-start(f32[4,360]{1,0:T(4,128)S(1)} %get-tuple-element.236) | copy-start | bytes 17284
  2.9 5.2 %copy-start.57 = (f32[4,360]{1,0:T(4,128)}, f32[4,360]{1,0:T(4,128)S(1)}, u32[]{:S(2)}) copy-start(f32[4,360]{1,0:T(4,128)S(1)} %get-tuple-element.242) | copy-start | bytes 17284
  2.9 5.2 %copy-start.58 = (f32[4,360]{1,0:T(4,128)}, f32[4,360]{1,0:T(4,128)S(1)}, u32[]{:S(2)}) copy-start(f32[4,360]{1,0:T(4,128)S(1)} %get-tuple-element.243) | copy-start | bytes 17284
  2.9 5.2 %copy-start.59 = (f32[4,360]{1,0:T(4,128)}, f32[4,360]{1,0:T(4,128)S(1)}, u32[]{:S(2)}) copy-start(f32[4,360]{1,0:T(4,128)S(1)} %get-tuple-element.244) | copy-start | bytes 17284
  9.8 42.3 %all-to-all-start = ((f32[4,128,360]{1,2,0:T(8,128)}), f32[4,128,360]{1,2,0:T(8,128)S(1)}, u32[]{:S(2)}, u32[]{:S(2)}) async-start(f32[4,128,360]{1,2,0:T(8,128)} %copy.52), calls=%async_computation | async-start | bytes 1474560 | tf_op jit(solution)/shard_map/all_to_all | solution.py:157
  13.8 56.5 %copy-start.16 = (s32[1440]{0:T(1024)}, s32[1440]{0:T(1024)S(1)}, u32[]{:S(2)}) copy-start(s32[1440]{0:T(1024)S(1)} %add_select_fusion.1) | copy-start | bytes 17284
  13.8 38.3 %copy-start.60 = (pred[1440]{0:T(1024)(128)(4,1)}, pred[1440]{0:T(1024)(128)(4,1)S(1)}, u32[]{:S(2)}) copy-start(pred[1440]{0:T(1024)(128)(4,1)S(1)} %get-tuple-element.272) | copy-start | bytes 4324
  13.9 56.4 %copy-start.62 = (pred[1440]{0:T(1024)(128)(4,1)}, pred[1440]{0:T(1024)(128)(4,1)S(1)}, u32[]{:S(2)}) copy-start(pred[1440]{0:T(1024)(128)(4,1)S(1)} %get-tuple-element.271) | copy-start | bytes 4324
  13.9 38.1 %copy-start.67 = (s32[4]{0:T(128)S(1)}, s32[4]{0:T(128)}, u32[]{:S(2)}) copy-start(s32[4]{0:T(128)} %param.19) | copy-start | bytes 52
  13.9 38.1 %copy-start.68 = (s32[4]{0:T(128)S(1)}, s32[4]{0:T(128)}, u32[]{:S(2)}) copy-start(s32[4]{0:T(128)} %param.18) | copy-start | bytes 52
  52.0 18.3 %copy-start.37 = (f32[1440]{0:T(1024)}, f32[1440]{0:T(1024)S(1)}, u32[]{:S(2)}) copy-start(f32[1440]{0:T(1024)S(1)} %select_multiply_fusion) | copy-start | bytes 17284
  52.1 18.2 %copy-start.65 = (s32[128]{0:T(128)}, s32[128]{0:T(128)S(1)}, u32[]{:S(2)}) copy-start(s32[128]{0:T(128)S(1)} %get-tuple-element.54) | copy-start | bytes 1540
  52.1 18.2 %copy-start.69 = (pred[128]{0:T(512)(128)(4,1)}, pred[128]{0:T(512)(128)(4,1)S(1)}, u32[]{:S(2)}) copy-start(pred[128]{0:T(512)(128)(4,1)S(1)} %broadcast_compare_fusion.3) | copy-start | bytes 388
  115.4 13.6 %all-to-all-start.1 = ((f32[4,128,360]{1,2,0:T(8,128)}), f32[4,128,360]{1,2,0:T(8,128)S(1)}, u32[]{:S(2)}, u32[]{:S(2)}) async-start(f32[4,128,360]{1,2,0:T(8,128)} %pad_maximum_fusion.8), calls=%async_computation.1 | async-start | bytes 1474560 | tf_op jit(solution)/shard_map/all_to_all | solution.py:181
  129.0 24.2 %copy-start.2 = (f32[4,128,360]{1,2,0:T(8,128)}, f32[4,128,360]{1,2,0:T(8,128)S(1)}, u32[]{:S(2)}) copy-start(f32[4,128,360]{1,2,0:T(8,128)S(1)} %all-to-all-done.1) | copy-start | bytes 2211844
  131.8 13.0 %collective-permute-start = (f32[3,360,160]{1,2,0:T(8,128)S(1)}, f32[3,360,160]{1,2,0:T(8,128)}, u32[]{:S(2)}, u32[]{:S(2)}) collective-permute-start(f32[3,360,160]{1,2,0:T(8,128)S(1)} %copy.54), channel_id=1, source_target_pairs={{0,1},{1,2},{2,3},{3,4},{4,5},{5,6},{6,7},{8,9},{9,10},{10,11},{11... | collective-permute-start | bytes 2073608 | tf_op jit(solution)/shard_map/ppermute | solution.py:29
  137.6 13.1 %collective-permute-start.1 = (f32[3,360,160]{1,2,0:T(8,128)}, f32[3,360,160]{1,2,0:T(8,128)}, u32[]{:S(2)}, u32[]{:S(2)}) collective-permute-start(f32[3,360,160]{1,2,0:T(8,128)} %copy.55), channel_id=1, source_target_pairs={{1,0},{2,1},{3,2},{4,3},{5,4},{6,5},{7,6},{9,8},{10,9},{11,10},{12... | collective-permute-start | bytes 2073608 | tf_op jit(solution)/shard_map/ppermute | solution.py:30
  173.0 25.5 %collective-permute-start.2 = (f32[6,360,128]{2,1,0:T(8,128)}, f32[6,360,128]{2,1,0:T(8,128)}, u32[]{:S(2)}, u32[]{:S(2)}) collective-permute-start(f32[6,360,128]{2,1,0:T(8,128)} %pad_maximum_fusion.6), channel_id=1, source_target_pairs={{0,16},{16,0},{8,24},{24,8},{1,17},{17,1},{9,25},{25,9},{2,18},{18... | collective-permute-start | bytes 3317768 | tf_op jit(solution)/shard_map/ppermute | solution.py:19
  200.7 3.5 collective-permute-start.3
  201.9 3.1 collective-permute-start.4
  217.5 7.2 %copy-start.17 = (s32[1440]{0:T(1024)S(1)}, s32[1440]{0:T(1024)}, u32[]{:S(2)}) copy-start(s32[1440]{0:T(1024)} %copy-done.16) | copy-start | bytes 17284
  217.5 7.2 %copy-start.63 = (pred[1440]{0:T(1024)(128)(4,1)S(1)}, pred[1440]{0:T(1024)(128)(4,1)}, u32[]{:S(2)}) copy-start(pred[1440]{0:T(1024)(128)(4,1)} %copy-done.62) | copy-start | bytes 4324
  220.8 42.0 %all-to-all-start.2 = ((f32[4,128,360]{1,2,0:T(8,128)}), f32[4,128,360]{1,2,0:T(8,128)S(1)}, u32[]{:S(2)}, u32[]{:S(2)}) async-start(f32[4,128,360]{1,2,0:T(8,128)} %copy.64), calls=%async_computation.2 | async-start | bytes 1474560 | tf_op jit(solution)/shard_map/all_to_all | solution.py:157
  224.7 38.1 %copy-start.38 = (f32[1440]{0:T(1024)S(1)}, f32[1440]{0:T(1024)}, u32[]{:S(2)}) copy-start(f32[1440]{0:T(1024)} %copy-done.37) | copy-start | bytes 17284
  224.7 38.1 %copy-start.61 = (pred[1440]{0:T(1024)(128)(4,1)S(1)}, pred[1440]{0:T(1024)(128)(4,1)}, u32[]{:S(2)}) copy-start(pred[1440]{0:T(1024)(128)(4,1)} %copy-done.60) | copy-start | bytes 4324
  224.7 38.1 %copy-start.66 = (s32[128]{0:T(128)S(1)}, s32[128]{0:T(128)}, u32[]{:S(2)}) copy-start(s32[128]{0:T(128)} %copy-done.65) | copy-start | bytes 1540
  262.8 18.1 %copy-start.70 = (pred[128]{0:T(512)(128)(4,1)S(1)}, pred[128]{0:T(512)(128)(4,1)}, u32[]{:S(2)}) copy-start(pred[128]{0:T(512)(128)(4,1)} %copy-done.69) | copy-start | bytes 388
  341.1 14.2 %collective-permute-start.5 = (f32[3,360,160]{1,2,0:T(8,128)S(1)}, f32[3,360,160]{1,2,0:T(8,128)}, u32[]{:S(2)}, u32[]{:S(2)}) collective-permute-start(f32[3,360,160]{1,2,0:T(8,128)S(1)} %copy.66), channel_id=1, source_target_pairs={{0,1},{1,2},{2,3},{3,4},{4,5},{5,6},{6,7},{8,9},{9,10},{10,11},{11... | collective-permute-start | bytes 2073608 | tf_op jit(solution)/shard_map/ppermute | solution.py:29
  349.4 13.1 %collective-permute-start.6 = (f32[3,360,160]{1,2,0:T(8,128)}, f32[3,360,160]{1,2,0:T(8,128)}, u32[]{:S(2)}, u32[]{:S(2)}) collective-permute-start(f32[3,360,160]{1,2,0:T(8,128)} %copy.67), channel_id=1, source_target_pairs={{1,0},{2,1},{3,2},{4,3},{5,4},{6,5},{7,6},{9,8},{10,9},{11,10},{12... | collective-permute-start | bytes 2073608 | tf_op jit(solution)/shard_map/ppermute | solution.py:30
  388.7 25.3 %collective-permute-start.7 = (f32[6,360,128]{2,1,0:T(8,128)S(1)}, f32[6,360,128]{2,1,0:T(8,128)S(1)}, u32[]{:S(2)}, u32[]{:S(2)}) collective-permute-start(f32[6,360,128]{2,1,0:T(8,128)S(1)} %pad_maximum_fusion.7), channel_id=1, source_target_pairs={{0,16},{16,0},{8,24},{24,8},{1,17},{17,1},{9,25},{25,9},{2,18},{18... | collective-permute-start | bytes 3317768 | tf_op jit(solution)/shard_map/ppermute | solution.py:19
  414.8 3.5 collective-permute-start.8
  415.4 3.0 collective-permute-start.9
  (20 other events, 52.2 us)
